TPU v7x, 32 devices: a whole 2x2x4 slice. The times are simulated.
32 devices in a mesh: freq: 8 (over y, x, core), row: 4 (over z).
Axes of the slice: x: 2, y: 2, z: 4, core: 2. Of those that a mesh axis runs over, the one named last changes fastest.
Arguments:
- source: bfloat16 [8, 2, 64, 512], P('freq', None, 'row'), may hold values from -6 to 6
- receiver: bfloat16 [8, 2, 64, 512], P('freq', None, 'row'), may hold values from -6 to 6
- filters: bfloat16 [8, 2, 2, 25, 25], P('freq'), may hold values from -0.15625 to 0.15625
- table_index: int32 [2, 64, 512], P(None, 'row'), may hold values from 0 to 1
- lags: int32 [16], replicated, may hold values from 0 to 15, each once
- offset_filters: float32 [16, 9, 9], P('freq'), may hold values from -0.15625 to 0.15625
Outputs:
- image: float32 [2, 16, 64, 512], P(None, 'freq', 'row')
Inputs may be any that keep to these rules, and one draw needn't show every extreme that they name: `lags`: each of 0 .. 15 appears exactly once.
All inputs are finite; a program needn't handle non-finite values.
Results may differ from a plain program's by a relative error of at most 0.0052.
Values may be sent and summed in bfloat16 or wider, within the bound.
A program may use at most 128 MiB of HBM per device.

v0:
```python
import functools

import jax
import jax.numpy as jnp
from jax import lax
from jax.experimental import pallas as pl
from jax.experimental.pallas import tpu as pltpu
from jax.sharding import PartitionSpec as P

MESH = pl.DeviceIdType.MESH
GROUP = 5
LANES = 128


def filter_matrix(taps, filt, rows):
    nv = taps.shape[0] // 2
    window = 3 * rows
    lead = rows - (filt - 1) // 2
    groups = -(-filt // GROUP)
    depth = -(-(GROUP * 2 * window) // LANES) * LANES
    at = lax.broadcasted_iota(jnp.int32, (taps.shape[2], depth), 1)
    first = lax.broadcasted_iota(jnp.int32, (taps.shape[2], depth), 0)
    section = lax.div(at, window)
    place = (at - section * window == first + lead) & (section < 2 * GROUP)
    place = place.astype(jnp.float32).astype(jnp.bfloat16)
    columns = taps.shape[1]
    first, section = first[:columns], section[:columns]
    kept = lax.rem(first, GROUP) == lax.div(section, 2)
    real_in = lax.rem(section, 2) == 0
    group_of = lax.div(lax.broadcasted_iota(jnp.int32, (groups * rows, columns), 0), rows)
    spread = lax.div(lax.broadcasted_iota(jnp.int32, (groups * rows, columns), 1), GROUP) == group_of
    spread = spread.astype(jnp.float32).astype(jnp.bfloat16)
    blocks = []
    for v in range(nv):
        real, imag = (
            jnp.where(kept, jnp.dot(taps[2 * v + i], place, preferred_element_type=jnp.float32), 0.0)
            for i in range(2)
        )
        for out in (jnp.where(real_in, real, -imag), jnp.where(real_in, imag, real)):
            blocks.append(jnp.dot(spread, out.astype(jnp.bfloat16), preferred_element_type=jnp.float32))
    tall = jnp.concatenate(
        [block[g * rows : (g + 1) * rows] for g in range(groups) for block in blocks], axis=0
    )
    row_ids = lax.rem(lax.broadcasted_iota(jnp.int32, tall.shape, 0), rows)
    move = 1
    while move < rows:
        tall = jnp.where(row_ids & move != 0, pltpu.roll(tall, move, 1), tall)
        move *= 2
    return tall.astype(jnp.bfloat16)


def kernel(
    nf,
    nr,
    filt,
    source,
    receiver,
    taps,
    index,
    lags,
    ofilters,
    image,
    matrix,
    shifted,
    field,
    halo,
    fsend,
    fgot,
    by_lag,
    rsend,
    rgot,
    plane,
    hs_sem,
    hr_sem,
    fs_sem,
    fr_sem,
    rs_sem,
    rr_sem,
    es_sem,
):
    depths, rows, width = index.shape
    noff = lags.shape[0]
    ofilt, kper, _ = ofilters.shape
    ohalf = (ofilt - 1) // 2
    per = rows // nf
    edge = ohalf // per
    wide = width + LANES
    groups = -(-filt // GROUP)
    nv = matrix.shape[0] // (groups * 2 * rows)

    f = lax.axis_index("freq")
    r = lax.axis_index("row")
    before, after = lax.rem(r + nr - 1, nr), lax.rem(r + 1, nr)
    has_left = r > 0
    has_right = r < nr - 1
    low = f < edge
    high = f >= nf - edge

    barrier = pltpu.get_barrier_semaphore()

    def greet(ff, rr):
        pl.semaphore_signal(barrier, inc=1, device_id=(ff, rr), device_id_type=MESH)

    @pl.when(has_left)
    def _():
        for p in range(nf - edge, nf):
            greet(p, before)

        @pl.when(f < nf - edge)
        def _():
            greet(f, before)

    @pl.when(has_right)
    def _():
        for p in range(edge):
            greet(p, after)

        @pl.when(f >= edge)
        def _():
            greet(f, after)

    for j in range(1, nf):
        greet(lax.rem(f + j, nf), r)

    def clear(side, first):
        for depth in range(depths):
            for g in range(2):
                for c in range(2):
                    halo[depth, side, g, c] = jnp.zeros((rows, width), halo.dtype)
            for p in range(edge):
                rgot[depth, first + p] = jnp.zeros(rgot.shape[2:], rgot.dtype)

    @pl.when(r < 1)
    def _():
        clear(0, 0)

    @pl.when(r >= nr - 1)
    def _():
        clear(1, edge + nf)

    pl.semaphore_wait(
        barrier,
        nf
        - 1
        + jnp.where(has_left, jnp.where(low, nf, 1), 0)
        + jnp.where(has_right, jnp.where(high, nf, 1), 0),
    )

    def halo_copy(depth, g, side, to):
        src = (source, receiver)[g].at[0] if depth == 0 else field.at[g]
        return pltpu.make_async_remote_copy(
            src_ref=src,
            dst_ref=halo.at[depth, side, g],
            send_sem=hs_sem.at[(depth * 2 + side) * 2 + g],
            recv_sem=hr_sem.at[(depth * 2 + side) * 2 + g],
            device_id=(f, to),
            device_id_type=MESH,
        )

    def halo_start(depth):
        @pl.when(has_right)
        def _():
            for g in range(2):
                halo_copy(depth, g, 0, after).start()

        @pl.when(has_left)
        def _():
            for g in range(2):
                halo_copy(depth, g, 1, before).start()

    def halo_recv(depth):
        @pl.when(has_left)
        def _():
            for g in range(2):
                halo_copy(depth, g, 0, before).wait_recv()

        @pl.when(has_right)
        def _():
            for g in range(2):
                halo_copy(depth, g, 1, after).wait_recv()

    def halo_sent(depth):
        @pl.when(has_right)
        def _():
            for g in range(2):
                halo_copy(depth, g, 0, after).wait_send()

        @pl.when(has_left)
        def _():
            for g in range(2):
                halo_copy(depth, g, 1, before).wait_send()

    def field_copy(depth, j):
        return pltpu.make_async_remote_copy(
            src_ref=fsend.at[depth, lax.rem(f + j, nf)],
            dst_ref=fgot.at[depth, j - 1],
            send_sem=fs_sem.at[depth * (nf - 1) + j - 1],
            recv_sem=fr_sem.at[depth * (nf - 1) + j - 1],
            device_id=(lax.rem(f + j, nf), r),
            device_id_type=MESH,
        )

    def raw_copy(depth, p, to, slot, sem):
        return pltpu.make_async_remote_copy(
            src_ref=rsend.at[depth, p],
            dst_ref=rgot.at[depth, slot],
            send_sem=sem,
            recv_sem=rr_sem.at[depth * (nf + 2 * edge) + slot],
            device_id=(p, to),
            device_id_type=MESH,
        )

    def raw_sends(depth, act):
        for j in range(1, nf):
            p = lax.rem(f + j, nf)
            act(raw_copy(depth, p, r, edge + f, rs_sem.at[depth * (nf - 1) + j - 1]))

        @pl.when(has_left)
        def _():
            @pl.when(low)
            def _():
                for p in range(nf):
                    act(raw_copy(depth, p, before, edge + nf + lax.rem(f, edge), es_sem.at[(depth * 2) * nf + p]))

        @pl.when(has_right)
        def _():
            @pl.when(high)
            def _():
                for p in range(nf):
                    slot = lax.rem(f + edge * nf - nf, edge)
                    act(raw_copy(depth, p, after, slot, es_sem.at[(depth * 2 + 1) * nf + p]))

    def raw_recv(depth):
        def wait(slot):
            raw_copy(depth, lax.rem(f + 1, nf), r, slot, rs_sem.at[depth * (nf - 1)]).wait_recv()

        for j in range(1, nf):
            wait(edge + lax.rem(f + j, nf))

        @pl.when(has_left)
        def _():
            for p in range(edge):
                wait(p)

        @pl.when(has_right)
        def _():
            for p in range(edge):
                wait(edge + nf + p)

    def filled(parts):
        count = sum(part.shape[0] for part in parts)
        if count % 8:
            parts = parts + [jnp.zeros((-count % 8, parts[0].shape[1]), parts[0].dtype)]
        return jnp.concatenate(parts, axis=0)

    def widen(value):
        zeros = jnp.zeros((value.shape[0], wide - width), value.dtype)
        return jnp.concatenate([value, zeros], axis=1)

    def step(depth):
        taken = jnp.concatenate([index[depth]] * 2, axis=0)
        window = 6 * rows
        for g in range(2):
            parts = []
            for c in range(2):
                part = c if g == 0 else 1 - c
                own = (source, receiver)[g][0, part] if depth == 0 else field[g, part]
                parts += [halo[depth, 0, g, part], own, halo[depth, 1, g, part]]
            tall = widen(jnp.concatenate(parts, axis=0).astype(jnp.float32))
            for b in range(GROUP):
                turn = (GROUP // 2 - b) % wide
                moved = pltpu.roll(tall, turn, 1) if turn else tall
                shifted[g, b * window : (b + 1) * window, :] = moved.astype(jnp.bfloat16)
        chosen = []
        for g in range(2):
            product = jnp.dot(matrix[...], shifted[g], preferred_element_type=jnp.float32)
            block = nv * 2 * rows
            total = None
            for b in range(groups):
                term = product[b * block : (b + 1) * block]
                turn = (-GROUP * (b - groups // 2)) % wide
                term = pltpu.roll(term, turn, 1) if turn else term
                total = term if total is None else total + term
            total = total[:, :width]
            out = total[: 2 * rows]
            for v in range(1, nv):
                out = jnp.where(taken == v, total[v * 2 * rows : (v + 1) * 2 * rows], out)
            chosen.append(out)
        return chosen

    def scatter_fields(depth, chosen):
        sections = [chosen[0][:rows], chosen[0][rows:], chosen[1][rows:], chosen[1][:rows]]
        for p in range(nf):
            piece = [s[p * per : (p + 1) * per] for s in sections]
            piece = filled(piece)
            piece = jnp.concatenate([piece[:, : width // 2], piece[:, width // 2 :]], axis=0)
            fsend[depth, p] = piece.astype(jnp.bfloat16)
        for j in range(1, nf):
            field_copy(depth, j).start()

    def correlate(depth):
        for j in range(1, nf):
            field_copy(depth, j).wait_recv()
        downs, ups = [], []
        for j in range(nf):
            piece = fsend[depth, f] if j == 0 else fgot[depth, j - 1]
            piece = piece.astype(jnp.float32)
            tile = piece.shape[0] // 2
            piece = jnp.concatenate([piece[:tile], piece[tile:]], axis=1)
            downs.append(piece[: 2 * per])
            ups.append(piece[2 * per : 4 * per])
        down = widen(jnp.concatenate(downs, axis=0))
        up = widen(jnp.concatenate(ups, axis=0))
        shift = noff // 2
        for lag in range(noff):
            offset = lag - shift
            turn = (-2 * offset) % wide
            terms = down * (pltpu.roll(up, turn, 1) if turn else up)
            total = terms[:8]
            for i in range(1, terms.shape[0] // 8):
                total = total + terms[8 * i : 8 * i + 8]
            turn = offset % wide
            total = (pltpu.roll(total, turn, 1) if turn else total)[:, :width]
            raw = total[:per]
            for i in range(1, 8 // per):
                raw = raw + total[i * per : (i + 1) * per]
            by_lag[lag] = filled([raw[:, : width // 2], raw[:, width // 2 :]])
        for p in range(nf):
            rsend[depth, p] = filled([by_lag[lags[p * kper + k]][: 2 * per] for k in range(kper)])
        raw_sends(depth, lambda copy: copy.start())
        rgot[depth, edge + f] = rsend[depth, f]

    def filter_images(depth):
        raw_recv(depth)
        pieces = [rgot[depth, s] for s in range(nf + 2 * edge)]
        for k in range(kper):
            left, right = (
                jnp.concatenate([piece[at : at + per] for piece in pieces], axis=0)
                for at in (2 * per * k, 2 * per * k + per)
            )
            plane[k] = widen(jnp.concatenate([left, right], axis=1))
        for k in range(kper):
            total = None
            for b in range(ofilt):
                column = None
                for a in range(ofilt):
                    term = ofilters[a, k, b] * plane[k, a : a + rows, :]
                    column = term if column is None else column + term
                turn = (ohalf - b) % wide
                column = (pltpu.roll(column, turn, 1) if turn else column)[:, :width]
                total = column if total is None else total + column
            image[depth, k] = total

    halo_start(0)

    matrix[...] = filter_matrix(taps, filt, rows)
    spare = shifted.shape[1] - GROUP * 6 * rows
    if spare:
        for g in range(2):
            shifted[g, GROUP * 6 * rows :, :] = jnp.zeros((spare, wide), jnp.bfloat16)

    halo_recv(0)
    for depth in range(depths):
        chosen = step(depth)
        if depth + 1 < depths:
            if depth:
                halo_sent(depth)
            for g in range(2):
                field[g, 0] = chosen[g][g * rows : (g + 1) * rows].astype(jnp.bfloat16)
                field[g, 1] = chosen[g][(1 - g) * rows : (2 - g) * rows].astype(jnp.bfloat16)
            halo_start(depth + 1)
        scatter_fields(depth, chosen)
        if depth + 1 < depths:
            halo_recv(depth + 1)
    for depth in range(depths):
        correlate(depth)
    for depth in range(depths):
        filter_images(depth)
    for depth in range(depths):
        if depth == 0 or depth + 1 == depths:
            halo_sent(depth)
        for j in range(1, nf):
            field_copy(depth, j).wait_send()
        raw_sends(depth, lambda copy: copy.wait_send())


def body(nf, nr, source, receiver, filters, table_index, lags, offset_filters):
    depths, rows, width = table_index.shape
    noff = lags.shape[0]
    kper, ofilt, _ = offset_filters.shape
    per = rows // nf
    edge = (ofilt - 1) // 2 // per
    wide = width + LANES
    nv, filt = filters.shape[1], filters.shape[3]
    taps = filters.transpose(0, 1, 2, 4, 3).reshape(nv * 2, filt, filt)
    taps = jnp.pad(taps, ((0, 0), (0, -filt % 32), (0, -filt % LANES)))
    groups = -(-filt // GROUP)
    contracted = -(-(GROUP * 6 * rows) // LANES) * LANES
    piece = -(-4 * per // 8) * 16
    image_piece = -(-2 * per * kper // 8) * 8
    half = width // 2
    vmem = pl.BlockSpec(memory_space=pltpu.VMEM)
    smem = pl.BlockSpec(memory_space=pltpu.SMEM)
    dma = pltpu.SemaphoreType.DMA
    return pl.pallas_call(
        functools.partial(kernel, nf, nr, filt),
        out_shape=jax.ShapeDtypeStruct((depths, kper, rows, width), jnp.float32),
        in_specs=[vmem, vmem, vmem, vmem, smem, smem],
        out_specs=vmem,
        scratch_shapes=[
            pltpu.VMEM((groups * nv * 2 * rows, contracted), jnp.bfloat16),
            pltpu.VMEM((2, contracted, wide), jnp.bfloat16),
            pltpu.VMEM((2, 2, rows, width), jnp.bfloat16),
            pltpu.VMEM((depths, 2, 2, 2, rows, width), jnp.bfloat16),
            pltpu.VMEM((depths, nf, piece, half), jnp.bfloat16),
            pltpu.VMEM((depths, nf - 1, piece, half), jnp.bfloat16),
            pltpu.VMEM((noff, -(-2 * per // 8) * 8, half), jnp.float32),
            pltpu.VMEM((depths, nf, image_piece, half), jnp.float32),
            pltpu.VMEM((depths, nf + 2 * edge, image_piece, half), jnp.float32),
            pltpu.VMEM((kper, rows + ofilt - 1, wide), jnp.float32),
            dma((depths * 4,)),
            dma((depths * 4,)),
            dma((depths * (nf - 1),)),
            dma((depths * (nf - 1),)),
            dma((depths * (nf - 1),)),
            dma((depths * (nf + 2 * edge),)),
            dma((depths * 2 * nf,)),
        ],
        compiler_params=pltpu.CompilerParams(
            collective_id=0, has_side_effects=True, vmem_limit_bytes=48 * 1024 * 1024
        ),
    )(source, receiver, taps, table_index, lags, offset_filters.transpose(1, 0, 2))


def solution(mesh):
    in_specs = (
        P("freq", None, "row", None),
        P("freq", None, "row", None),
        P("freq", None, None, None, None),
        P(None, "row", None),
        P(),
        P("freq", None, None),
    )
    out_specs = P(None, "freq", "row", None)
    return jax.shard_map(
        functools.partial(body, mesh.shape["freq"], mesh.shape["row"]),
        mesh=mesh,
        in_specs=in_specs,
        out_specs=out_specs,
        check_vma=False,
    )
```

profile of v0, /device:TPU:0, one launch (start us, length us, event | category | flops | bytes accessed | tf_op | source)
XLA Modules:
  0.0 26.4 jit_solution(2424509143204902453)
XLA Ops:
  0.0 0.0 copy-start
  0.0 0.9 %copy.7 = bf16[1,2,2,25,25]{4,3,2,1,0:T(8,128)(2,1)S(1)} copy(bf16[1,2,2,25,25]{3,2,4,1,0:T(2,128)(2,1)} %bitcast.5) | data formatting | bytes 10000 | tf_op jit(solution)/shard_map/transpose | solution.py:395
  0.9 0.0 copy-start.1
  0.9 0.0 copy-start.3
  0.9 0.0 copy-start.4
  0.9 0.0 copy-done
  1.0 0.7 %copy-done.1 = bf16[1,2,16,512]{3,2,1,0:T(8,128)(2,1)S(1)} copy-done((bf16[1,2,16,512]{3,2,1,0:T(8,128)(2,1)S(1)}, bf16[1,2,16,512]{3,2,1,0:T(8,128)(2,1)}, u32[]{:S(2)}) %copy-start.1) | copy-done | bytes 32792
  1.7 0.0 copy-done.3
  1.7 0.0 copy-done.4
  1.7 0.0 copy-start.2
  1.7 0.8 %copy-done.2 = bf16[1,2,16,512]{3,2,1,0:T(8,128)(2,1)S(1)} copy-done((bf16[1,2,16,512]{3,2,1,0:T(8,128)(2,1)S(1)}, bf16[1,2,16,512]{3,2,1,0:T(8,128)(2,1)}, u32[]{:S(2)}) %copy-start.2) | copy-done | bytes 32792
  2.4 23.3 %shard_map.64 = f32[2,2,16,512]{3,2,1,0:T(8,128)S(1)} custom-call(bf16[1,2,16,512]{3,2,1,0:T(8,128)(2,1)S(1)} %copy-done.1, bf16[1,2,16,512]{3,2,1,0:T(8,128)(2,1)S(1)} %copy-done.2, bf16[4,32,128]{2,1,0:T(8,128)(2,1)S(1)} %pad.4.taps, s32[2,16,512]{2,1,0:T(8,128)S(1)} %copy-done, s32[16]{0:T(128)S(1)} %copy-done.4, f32[9,2,9]{2,1,0:T(2,128)S(1)} %bitcast.3), custom_call_target="tpu_custom_call" | custom-call | tf_op jit(solution)/shard_map/pallas_call | solution.py:405
  25.8 0.7 %copy.9 = f32[2,2,16,512]{3,2,1,0:T(8,128)} copy(f32[2,2,16,512]{3,2,1,0:T(8,128)S(1)} %shard_map.64) | data formatting | bytes 262144
  (1 shorter events, 0.0 us)
Async XLA Ops:
  0.0 0.9 %copy-start = (s32[2,16,512]{2,1,0:T(8,128)S(1)}, s32[2,16,512]{2,1,0:T(8,128)}, u32[]{:S(2)}) copy-start(s32[2,16,512]{2,1,0:T(8,128)} %index.1) | copy-start | bytes 196612
  0.9 0.8 %copy-start.1 = (bf16[1,2,16,512]{3,2,1,0:T(8,128)(2,1)S(1)}, bf16[1,2,16,512]{3,2,1,0:T(8,128)(2,1)}, u32[]{:S(2)}) copy-start(bf16[1,2,16,512]{3,2,1,0:T(8,128)(2,1)} %source.1) | copy-start | bytes 98308
  0.9 0.8 %copy-start.3 = (f32[2,9,9]{2,0,1:T(2,128)S(1)}, f32[2,9,9]{2,0,1:T(2,128)}, u32[]{:S(2)}) copy-start(f32[2,9,9]{2,0,1:T(2,128)} %param.11) | copy-start | bytes 1948
  0.9 0.8 %copy-start.4 = (s32[16]{0:T(128)S(1)}, s32[16]{0:T(128)}, u32[]{:S(2)}) copy-start(s32[16]{0:T(128)} %lags.1) | copy-start | bytes 196
  1.7 0.8 %copy-start.2 = (bf16[1,2,16,512]{3,2,1,0:T(8,128)(2,1)S(1)}, bf16[1,2,16,512]{3,2,1,0:T(8,128)(2,1)}, u32[]{:S(2)}) copy-start(bf16[1,2,16,512]{3,2,1,0:T(8,128)(2,1)} %receiver.1) | copy-start | bytes 98308
where the time goes:
time: 26.7 us; the launch traced here: 26.4 us
  Pallas kernels  23.3 us (87%)
  local copies, waits for them, and re-layouts  3.04 us (11%)
    pallas_call x1, Pallas kernels, body(): pl.pallas_call(functools.partial(kernel, nf, nr, filt), out_shape=jax.Sha...  23.3 us
    unnamed x11, local copies, waits for them, and re-layouts  2.14 us
    transpose x1, local copies, waits for them, and re-layouts, body(): taps = filters.transpose(0, 1, 2, 4, 3).reshape(nv * 2, filt, filt)  0.89 us

commit v1 on v0

--- a/solution.py
+++ b/solution.py
@@ -10,6 +10,7 @@
 MESH = pl.DeviceIdType.MESH
 GROUP = 5
 LANES = 128
+ROLLED = jnp.bfloat16
 
 
 def filter_matrix(taps, filt, rows):
@@ -60,6 +61,7 @@
     lags,
     ofilters,
     image,
+    table,
     matrix,
     shifted,
     field,
@@ -77,6 +79,7 @@
     rs_sem,
     rr_sem,
     es_sem,
+    in_sem,
 ):
     depths, rows, width = index.shape
     noff = lags.shape[0]
@@ -96,6 +99,14 @@
     low = f < edge
     high = f >= nf - edge
 
+    loads = [
+        pltpu.make_async_copy(source.at[0], field.at[0, 0], in_sem.at[0]),
+        pltpu.make_async_copy(receiver.at[0], field.at[0, 1], in_sem.at[1]),
+        pltpu.make_async_copy(index, table, in_sem.at[2]),
+    ]
+    for load in loads:
+        load.start()
+
     barrier = pltpu.get_barrier_semaphore()
 
     def greet(ff, rr):
@@ -147,7 +158,7 @@
     )
 
     def halo_copy(depth, g, side, to):
-        src = (source, receiver)[g].at[0] if depth == 0 else field.at[g]
+        src = (source, receiver)[g].at[0] if depth == 0 else field.at[depth, g]
         return pltpu.make_async_remote_copy(
             src_ref=src,
             dst_ref=halo.at[depth, side, g],
@@ -157,38 +168,32 @@
             device_id_type=MESH,
         )
 
-    def halo_start(depth):
+    def halo_start(depth, g):
         @pl.when(has_right)
         def _():
-            for g in range(2):
-                halo_copy(depth, g, 0, after).start()
+            halo_copy(depth, g, 0, after).start()
 
         @pl.when(has_left)
         def _():
-            for g in range(2):
-                halo_copy(depth, g, 1, before).start()
-
-    def halo_recv(depth):
+            halo_copy(depth, g, 1, before).start()
+
+    def halo_recv(depth, g):
         @pl.when(has_left)
         def _():
-            for g in range(2):
-                halo_copy(depth, g, 0, before).wait_recv()
+            halo_copy(depth, g, 0, before).wait_recv()
 
         @pl.when(has_right)
         def _():
-            for g in range(2):
-                halo_copy(depth, g, 1, after).wait_recv()
-
-    def halo_sent(depth):
+            halo_copy(depth, g, 1, after).wait_recv()
+
+    def halo_sent(depth, g):
         @pl.when(has_right)
         def _():
-            for g in range(2):
-                halo_copy(depth, g, 0, after).wait_send()
+            halo_copy(depth, g, 0, after).wait_send()
 
         @pl.when(has_left)
         def _():
-            for g in range(2):
-                halo_copy(depth, g, 1, before).wait_send()
+            halo_copy(depth, g, 1, before).wait_send()
 
     def field_copy(depth, j):
         return pltpu.make_async_remote_copy(
@@ -257,36 +262,31 @@
         zeros = jnp.zeros((value.shape[0], wide - width), value.dtype)
         return jnp.concatenate([value, zeros], axis=1)
 
-    def step(depth):
-        taken = jnp.concatenate([index[depth]] * 2, axis=0)
+    def step(depth, g):
+        taken = jnp.concatenate([table[depth]] * 2, axis=0)
         window = 6 * rows
-        for g in range(2):
-            parts = []
-            for c in range(2):
-                part = c if g == 0 else 1 - c
-                own = (source, receiver)[g][0, part] if depth == 0 else field[g, part]
-                parts += [halo[depth, 0, g, part], own, halo[depth, 1, g, part]]
-            tall = widen(jnp.concatenate(parts, axis=0).astype(jnp.float32))
-            for b in range(GROUP):
-                turn = (GROUP // 2 - b) % wide
-                moved = pltpu.roll(tall, turn, 1) if turn else tall
-                shifted[g, b * window : (b + 1) * window, :] = moved.astype(jnp.bfloat16)
-        chosen = []
-        for g in range(2):
-            product = jnp.dot(matrix[...], shifted[g], preferred_element_type=jnp.float32)
-            block = nv * 2 * rows
-            total = None
-            for b in range(groups):
-                term = product[b * block : (b + 1) * block]
-                turn = (-GROUP * (b - groups // 2)) % wide
-                term = pltpu.roll(term, turn, 1) if turn else term
-                total = term if total is None else total + term
-            total = total[:, :width]
-            out = total[: 2 * rows]
-            for v in range(1, nv):
-                out = jnp.where(taken == v, total[v * 2 * rows : (v + 1) * 2 * rows], out)
-            chosen.append(out)
-        return chosen
+        parts = []
+        for c in range(2):
+            part = c if g == 0 else 1 - c
+            parts += [halo[depth, 0, g, part], field[depth, g, part], halo[depth, 1, g, part]]
+        tall = widen(jnp.concatenate(parts, axis=0).astype(ROLLED))
+        for b in range(GROUP):
+            turn = (GROUP // 2 - b) % wide
+            moved = pltpu.roll(tall, turn, 1) if turn else tall
+            shifted[g, b * window : (b + 1) * window, :] = moved.astype(jnp.bfloat16)
+        product = jnp.dot(matrix[...], shifted[g], preferred_element_type=jnp.float32)
+        block = nv * 2 * rows
+        total = None
+        for b in range(groups):
+            term = product[b * block : (b + 1) * block]
+            turn = (-GROUP * (b - groups // 2)) % wide
+            term = pltpu.roll(term, turn, 1) if turn else term
+            total = term if total is None else total + term
+        total = total[:, :width]
+        out = total[: 2 * rows]
+        for v in range(1, nv):
+            out = jnp.where(taken == v, total[v * 2 * rows : (v + 1) * 2 * rows], out)
+        return out
 
     def scatter_fields(depth, chosen):
         sections = [chosen[0][:rows], chosen[0][rows:], chosen[1][rows:], chosen[1][:rows]]
@@ -340,18 +340,23 @@
             )
             plane[k] = widen(jnp.concatenate([left, right], axis=1))
         for k in range(kper):
-            total = None
-            for b in range(ofilt):
-                column = None
+            for top in range(0, rows, 8):
+                columns = [None] * ofilt
                 for a in range(ofilt):
-                    term = ofilters[a, k, b] * plane[k, a : a + rows, :]
-                    column = term if column is None else column + term
-                turn = (ohalf - b) % wide
-                column = (pltpu.roll(column, turn, 1) if turn else column)[:, :width]
-                total = column if total is None else total + column
-            image[depth, k] = total
-
-    halo_start(0)
+                    lines = plane[k, top + a : top + a + 8, :]
+                    for b in range(ofilt):
+                        term = ofilters[a, k, b] * lines
+                        columns[b] = term if a == 0 else columns[b] + term
+                total = None
+                for b in range(ofilt):
+                    turn = (ohalf - b) % wide
+                    column = pltpu.roll(columns[b], turn, 1) if turn else columns[b]
+                    column = column[:, :width]
+                    total = column if total is None else total + column
+                image[depth, k, top : top + 8, :] = total
+
+    halo_start(0, 0)
+    halo_start(0, 1)
 
     matrix[...] = filter_matrix(taps, filt, rows)
     spare = shifted.shape[1] - GROUP * 6 * rows
@@ -359,26 +364,28 @@
         for g in range(2):
             shifted[g, GROUP * 6 * rows :, :] = jnp.zeros((spare, wide), jnp.bfloat16)
 
-    halo_recv(0)
     for depth in range(depths):
-        chosen = step(depth)
-        if depth + 1 < depths:
-            if depth:
-                halo_sent(depth)
-            for g in range(2):
-                field[g, 0] = chosen[g][g * rows : (g + 1) * rows].astype(jnp.bfloat16)
-                field[g, 1] = chosen[g][(1 - g) * rows : (2 - g) * rows].astype(jnp.bfloat16)
-            halo_start(depth + 1)
+        chosen = []
+        for g in range(2):
+            if depth == 0:
+                loads[g].wait()
+                if g == 0:
+                    loads[2].wait()
+            halo_recv(depth, g)
+            out = step(depth, g)
+            if depth + 1 < depths:
+                field[depth + 1, g, 0] = out[g * rows : (g + 1) * rows].astype(jnp.bfloat16)
+                field[depth + 1, g, 1] = out[(1 - g) * rows : (2 - g) * rows].astype(jnp.bfloat16)
+                halo_start(depth + 1, g)
+            chosen.append(out)
         scatter_fields(depth, chosen)
-        if depth + 1 < depths:
-            halo_recv(depth + 1)
     for depth in range(depths):
         correlate(depth)
     for depth in range(depths):
         filter_images(depth)
     for depth in range(depths):
-        if depth == 0 or depth + 1 == depths:
-            halo_sent(depth)
+        for g in range(2):
+            halo_sent(depth, g)
         for j in range(1, nf):
             field_copy(depth, j).wait_send()
         raw_sends(depth, lambda copy: copy.wait_send())
@@ -400,17 +407,19 @@
     image_piece = -(-2 * per * kper // 8) * 8
     half = width // 2
     vmem = pl.BlockSpec(memory_space=pltpu.VMEM)
+    far = pl.BlockSpec(memory_space=pl.ANY)
     smem = pl.BlockSpec(memory_space=pltpu.SMEM)
     dma = pltpu.SemaphoreType.DMA
     return pl.pallas_call(
         functools.partial(kernel, nf, nr, filt),
         out_shape=jax.ShapeDtypeStruct((depths, kper, rows, width), jnp.float32),
-        in_specs=[vmem, vmem, vmem, vmem, smem, smem],
+        in_specs=[far, far, vmem, far, smem, smem],
         out_specs=vmem,
         scratch_shapes=[
+            pltpu.VMEM(table_index.shape, jnp.int32),
             pltpu.VMEM((groups * nv * 2 * rows, contracted), jnp.bfloat16),
             pltpu.VMEM((2, contracted, wide), jnp.bfloat16),
-            pltpu.VMEM((2, 2, rows, width), jnp.bfloat16),
+            pltpu.VMEM((depths, 2, 2, rows, width), jnp.bfloat16),
             pltpu.VMEM((depths, 2, 2, 2, rows, width), jnp.bfloat16),
             pltpu.VMEM((depths, nf, piece, half), jnp.bfloat16),
             pltpu.VMEM((depths, nf - 1, piece, half), jnp.bfloat16),
@@ -425,9 +434,10 @@
             dma((depths * (nf - 1),)),
             dma((depths * (nf + 2 * edge),)),
             dma((depths * 2 * nf,)),
+            dma((3,)),
         ],
         compiler_params=pltpu.CompilerParams(
-            collective_id=0, has_side_effects=True, vmem_limit_bytes=48 * 1024 * 1024
+            collective_id=0, has_side_effects=True, vmem_limit_bytes=60 * 1024 * 1024
         ),
     )(source, receiver, taps, table_index, lags, offset_filters.transpose(1, 0, 2))
 

time: 26.7 us -> 27.4 us (1.026)
  Pallas kernels: 23.3 us -> 24.1 us
    pallas_call x1, Pallas kernels: 23.3 us -> 24.1 us  [body(): pl.pallas_call(functools.partial(kernel, nf, nr, filt), out_shape=jax.Sha...]
    pad x1, local copies, waits for them, and re-layouts: 0.01 us -> 0.63 us  [body(): taps = jnp.pad(taps, ((0, 0), (0, -filt % 32), (0, -filt % LANES)))]
    unnamed x11 -> x1, local copies, waits for them, and re-layouts: 2.14 us -> 1.57 us
where the time goes in v1:
time: 27.4 us; the launch traced here: 27.2 us
  Pallas kernels  24.1 us (88%)
  local copies, waits for them, and re-layouts  3.06 us (11%)
    pallas_call x1, Pallas kernels, body(): pl.pallas_call(functools.partial(kernel, nf, nr, filt), out_shape=jax.Sha...  24.1 us
    unnamed x1, local copies, waits for them, and re-layouts  1.57 us
    transpose x1, local copies, waits for them, and re-layouts, body(): taps = filters.transpose(0, 1, 2, 4, 3).reshape(nv * 2, filt, filt)  0.86 us
    pad x1, local copies, waits for them, and re-layouts, body(): taps = jnp.pad(taps, ((0, 0), (0, -filt % 32), (0, -filt % LANES)))  0.63 us

profile of v1, /device:TPU:0, one launch (start us, length us, event | category | flops | bytes accessed | tf_op | source)
XLA Modules:
  0.0 27.2 jit_solution(692869450322704654)
XLA Ops:
  0.0 0.9 %copy.7 = bf16[1,2,2,25,25]{4,3,2,1,0:T(8,128)(2,1)S(1)} copy(bf16[1,2,2,25,25]{3,2,4,1,0:T(2,128)(2,1)} %bitcast.4) | data formatting | bytes 10000 | tf_op jit(solution)/shard_map/transpose | solution.py:402
  0.9 0.6 %pad.4.taps = bf16[4,32,128]{2,1,0:T(8,128)(2,1)} pad(bf16[4,25,25]{2,1,0:T(8,128)(2,1)S(1)} %bitcast.3, bf16[]{:T(256)} %constant.2.clone.1), padding=0_0x0_7x0_103 | pad | bytes 37770 | tf_op jit(solution)/shard_map/jit(_pad)/pad | solution.py:403
  1.5 24.1 %shard_map.64 = f32[2,2,16,512]{3,2,1,0:T(8,128)} custom-call(bf16[1,2,16,512]{3,2,1,0:T(8,128)(2,1)} %source.1, bf16[1,2,16,512]{3,2,1,0:T(8,128)(2,1)} %receiver.1, bf16[4,32,128]{2,1,0:T(8,128)(2,1)} %pad.4.taps, s32[2,16,512]{2,1,0:T(8,128)} %index.1, s32[16]{0:T(128)} %lags.1, f32[9,2,9]{2,1,0:T(2,128)} %bitcast.5), custom_call_target="tpu_custom_call" | custom-call | tf_op jit(solution)/shard_map/pallas_call | solution.py:413
  25.6 1.6 %copy.9 = f32[2,2,16,512]{3,2,1,0:T(8,128)} copy(f32[2,2,16,512]{3,2,1,0:T(8,128)} %shard_map.64) | data formatting | bytes 262144

commit v2 on v1

--- a/solution.py
+++ b/solution.py
@@ -61,7 +61,6 @@
     lags,
     ofilters,
     image,
-    table,
     matrix,
     shifted,
     field,
@@ -79,7 +78,6 @@
     rs_sem,
     rr_sem,
     es_sem,
-    in_sem,
 ):
     depths, rows, width = index.shape
     noff = lags.shape[0]
@@ -99,14 +97,6 @@
     low = f < edge
     high = f >= nf - edge
 
-    loads = [
-        pltpu.make_async_copy(source.at[0], field.at[0, 0], in_sem.at[0]),
-        pltpu.make_async_copy(receiver.at[0], field.at[0, 1], in_sem.at[1]),
-        pltpu.make_async_copy(index, table, in_sem.at[2]),
-    ]
-    for load in loads:
-        load.start()
-
     barrier = pltpu.get_barrier_semaphore()
 
     def greet(ff, rr):
@@ -158,7 +148,7 @@
     )
 
     def halo_copy(depth, g, side, to):
-        src = (source, receiver)[g].at[0] if depth == 0 else field.at[depth, g]
+        src = (source, receiver)[g].at[0] if depth == 0 else field.at[depth - 1, g]
         return pltpu.make_async_remote_copy(
             src_ref=src,
             dst_ref=halo.at[depth, side, g],
@@ -216,10 +206,6 @@
         )
 
     def raw_sends(depth, act):
-        for j in range(1, nf):
-            p = lax.rem(f + j, nf)
-            act(raw_copy(depth, p, r, edge + f, rs_sem.at[depth * (nf - 1) + j - 1]))
-
         @pl.when(has_left)
         def _():
             @pl.when(low)
@@ -235,6 +221,10 @@
                     slot = lax.rem(f + edge * nf - nf, edge)
                     act(raw_copy(depth, p, after, slot, es_sem.at[(depth * 2 + 1) * nf + p]))
 
+        for j in range(1, nf):
+            p = lax.rem(f + j, nf)
+            act(raw_copy(depth, p, r, edge + f, rs_sem.at[depth * (nf - 1) + j - 1]))
+
     def raw_recv(depth):
         def wait(slot):
             raw_copy(depth, lax.rem(f + 1, nf), r, slot, rs_sem.at[depth * (nf - 1)]).wait_recv()
@@ -263,12 +253,13 @@
         return jnp.concatenate([value, zeros], axis=1)
 
     def step(depth, g):
-        taken = jnp.concatenate([table[depth]] * 2, axis=0)
+        taken = jnp.concatenate([index[depth]] * 2, axis=0)
         window = 6 * rows
         parts = []
         for c in range(2):
             part = c if g == 0 else 1 - c
-            parts += [halo[depth, 0, g, part], field[depth, g, part], halo[depth, 1, g, part]]
+            own = (source, receiver)[g][0, part] if depth == 0 else field[depth - 1, g, part]
+            parts += [halo[depth, 0, g, part], own, halo[depth, 1, g, part]]
         tall = widen(jnp.concatenate(parts, axis=0).astype(ROLLED))
         for b in range(GROUP):
             turn = (GROUP // 2 - b) % wide
@@ -367,15 +358,11 @@
     for depth in range(depths):
         chosen = []
         for g in range(2):
-            if depth == 0:
-                loads[g].wait()
-                if g == 0:
-                    loads[2].wait()
             halo_recv(depth, g)
             out = step(depth, g)
             if depth + 1 < depths:
-                field[depth + 1, g, 0] = out[g * rows : (g + 1) * rows].astype(jnp.bfloat16)
-                field[depth + 1, g, 1] = out[(1 - g) * rows : (2 - g) * rows].astype(jnp.bfloat16)
+                field[depth, g, 0] = out[g * rows : (g + 1) * rows].astype(jnp.bfloat16)
+                field[depth, g, 1] = out[(1 - g) * rows : (2 - g) * rows].astype(jnp.bfloat16)
                 halo_start(depth + 1, g)
             chosen.append(out)
         scatter_fields(depth, chosen)
@@ -407,16 +394,14 @@
     image_piece = -(-2 * per * kper // 8) * 8
     half = width // 2
     vmem = pl.BlockSpec(memory_space=pltpu.VMEM)
-    far = pl.BlockSpec(memory_space=pl.ANY)
     smem = pl.BlockSpec(memory_space=pltpu.SMEM)
     dma = pltpu.SemaphoreType.DMA
     return pl.pallas_call(
         functools.partial(kernel, nf, nr, filt),
         out_shape=jax.ShapeDtypeStruct((depths, kper, rows, width), jnp.float32),
-        in_specs=[far, far, vmem, far, smem, smem],
+        in_specs=[vmem, vmem, vmem, vmem, smem, smem],
         out_specs=vmem,
         scratch_shapes=[
-            pltpu.VMEM(table_index.shape, jnp.int32),
             pltpu.VMEM((groups * nv * 2 * rows, contracted), jnp.bfloat16),
             pltpu.VMEM((2, contracted, wide), jnp.bfloat16),
             pltpu.VMEM((depths, 2, 2, rows, width), jnp.bfloat16),
@@ -434,10 +419,9 @@
             dma((depths * (nf - 1),)),
             dma((depths * (nf + 2 * edge),)),
             dma((depths * 2 * nf,)),
-            dma((3,)),
         ],
         compiler_params=pltpu.CompilerParams(
-            collective_id=0, has_side_effects=True, vmem_limit_bytes=60 * 1024 * 1024
+            collective_id=0, has_side_effects=True, vmem_limit_bytes=48 * 1024 * 1024
         ),
     )(source, receiver, taps, table_index, lags, offset_filters.transpose(1, 0, 2))
 

time: 27.4 us -> 26.5 us (0.967)
  Pallas kernels: 24.1 us -> 23.2 us
    pallas_call x1, Pallas kernels: 24.1 us -> 23.2 us  [body(): pl.pallas_call(functools.partial(kernel, nf, nr, filt), out_shape=jax.Sha...]
    pad x1, local copies, waits for them, and re-layouts: 0.63 us -> 0.01 us  [body(): taps = jnp.pad(taps, ((0, 0), (0, -filt % 32), (0, -filt % LANES)))]
    unnamed x1 -> x11, local copies, waits for them, and re-layouts: 1.57 us -> 2.14 us
where the time goes in v2:
time: 26.5 us; the launch traced here: 26.3 us
  Pallas kernels  23.2 us (88%)
  local copies, waits for them, and re-layouts  3.04 us (11%)
    pallas_call x1, Pallas kernels, body(): pl.pallas_call(functools.partial(kernel, nf, nr, filt), out_shape=jax.Sha...  23.2 us
    unnamed x11, local copies, waits for them, and re-layouts  2.14 us
    transpose x1, local copies, waits for them, and re-layouts, body(): taps = filters.transpose(0, 1, 2, 4, 3).reshape(nv * 2, filt, filt)  0.89 us

profile of v2, /device:TPU:0, one launch (start us, length us, event | category | flops | bytes accessed | tf_op | source)
XLA Modules:
  0.0 26.3 jit_solution(889921824578863489)
XLA Ops:
  0.0 0.0 copy-start
  0.0 0.9 %copy.7 = bf16[1,2,2,25,25]{4,3,2,1,0:T(8,128)(2,1)S(1)} copy(bf16[1,2,2,25,25]{3,2,4,1,0:T(2,128)(2,1)} %bitcast.5) | data formatting | bytes 10000 | tf_op jit(solution)/shard_map/transpose | solution.py:389
  0.9 0.0 copy-start.1
  0.9 0.0 copy-start.3
  0.9 0.0 copy-start.4
  0.9 0.0 copy-done
  1.0 0.7 %copy-done.1 = bf16[1,2,16,512]{3,2,1,0:T(8,128)(2,1)S(1)} copy-done((bf16[1,2,16,512]{3,2,1,0:T(8,128)(2,1)S(1)}, bf16[1,2,16,512]{3,2,1,0:T(8,128)(2,1)}, u32[]{:S(2)}) %copy-start.1) | copy-done | bytes 32792
  1.7 0.0 copy-done.3
  1.7 0.0 copy-done.4
  1.7 0.0 copy-start.2
  1.7 0.8 %copy-done.2 = bf16[1,2,16,512]{3,2,1,0:T(8,128)(2,1)S(1)} copy-done((bf16[1,2,16,512]{3,2,1,0:T(8,128)(2,1)S(1)}, bf16[1,2,16,512]{3,2,1,0:T(8,128)(2,1)}, u32[]{:S(2)}) %copy-start.2) | copy-done | bytes 32792
  2.4 23.2 %shard_map.64 = f32[2,2,16,512]{3,2,1,0:T(8,128)S(1)} custom-call(bf16[1,2,16,512]{3,2,1,0:T(8,128)(2,1)S(1)} %copy-done.1, bf16[1,2,16,512]{3,2,1,0:T(8,128)(2,1)S(1)} %copy-done.2, bf16[4,32,128]{2,1,0:T(8,128)(2,1)S(1)} %pad.4.taps, s32[2,16,512]{2,1,0:T(8,128)S(1)} %copy-done, s32[16]{0:T(128)S(1)} %copy-done.4, f32[9,2,9]{2,1,0:T(2,128)S(1)} %bitcast.3), custom_call_target="tpu_custom_call" | custom-call | tf_op jit(solution)/shard_map/pallas_call | solution.py:399
  25.6 0.7 %copy.9 = f32[2,2,16,512]{3,2,1,0:T(8,128)} copy(f32[2,2,16,512]{3,2,1,0:T(8,128)S(1)} %shard_map.64) | data formatting | bytes 262144
  (1 shorter events, 0.0 us)
Async XLA Ops:
  0.0 0.9 %copy-start = (s32[2,16,512]{2,1,0:T(8,128)S(1)}, s32[2,16,512]{2,1,0:T(8,128)}, u32[]{:S(2)}) copy-start(s32[2,16,512]{2,1,0:T(8,128)} %index.1) | copy-start | bytes 196612
  0.9 0.8 %copy-start.1 = (bf16[1,2,16,512]{3,2,1,0:T(8,128)(2,1)S(1)}, bf16[1,2,16,512]{3,2,1,0:T(8,128)(2,1)}, u32[]{:S(2)}) copy-start(bf16[1,2,16,512]{3,2,1,0:T(8,128)(2,1)} %source.1) | copy-start | bytes 98308
  0.9 0.8 %copy-start.3 = (f32[2,9,9]{2,0,1:T(2,128)S(1)}, f32[2,9,9]{2,0,1:T(2,128)}, u32[]{:S(2)}) copy-start(f32[2,9,9]{2,0,1:T(2,128)} %param.11) | copy-start | bytes 1948
  0.9 0.8 %copy-start.4 = (s32[16]{0:T(128)S(1)}, s32[16]{0:T(128)}, u32[]{:S(2)}) copy-start(s32[16]{0:T(128)} %lags.1) | copy-start | bytes 196
  1.7 0.8 %copy-start.2 = (bf16[1,2,16,512]{3,2,1,0:T(8,128)(2,1)S(1)}, bf16[1,2,16,512]{3,2,1,0:T(8,128)(2,1)}, u32[]{:S(2)}) copy-start(bf16[1,2,16,512]{3,2,1,0:T(8,128)(2,1)} %receiver.1) | copy-start | bytes 98308

commit v3 on v2

--- a/solution.py
+++ b/solution.py
@@ -365,11 +365,13 @@
                 field[depth, g, 1] = out[(1 - g) * rows : (2 - g) * rows].astype(jnp.bfloat16)
                 halo_start(depth + 1, g)
             chosen.append(out)
+            if g == 0 and depth:
+                correlate(depth - 1)
         scatter_fields(depth, chosen)
-    for depth in range(depths):
-        correlate(depth)
-    for depth in range(depths):
-        filter_images(depth)
+        if depth:
+            filter_images(depth - 1)
+    correlate(depths - 1)
+    filter_images(depths - 1)
     for depth in range(depths):
         for g in range(2):
             halo_sent(depth, g)

time: 26.5 us -> 29.3 us (1.11)
  Pallas kernels: 23.2 us -> 25.9 us
    pallas_call x1, Pallas kernels: 23.2 us -> 25.9 us  [body(): pl.pallas_call(functools.partial(kernel, nf, nr, filt), out_shape=jax.Sha...]
where the time goes in v3:
time: 29.3 us; the launch traced here: 29 us
  Pallas kernels  25.9 us (88%)
  local copies, waits for them, and re-layouts  3.04 us (10%)
    pallas_call x1, Pallas kernels, body(): pl.pallas_call(functools.partial(kernel, nf, nr, filt), out_shape=jax.Sha...  25.9 us
    unnamed x11, local copies, waits for them, and re-layouts  2.14 us
    transpose x1, local copies, waits for them, and re-layouts, body(): taps = filters.transpose(0, 1, 2, 4, 3).reshape(nv * 2, filt, filt)  0.89 us

profile of v3, /device:TPU:0, one launch (start us, length us, event | category | flops | bytes accessed | tf_op | source)
XLA Modules:
  0.0 29.0 jit_solution(13452279441462148512)
XLA Ops:
  0.0 0.0 copy-start
  0.0 0.9 %copy.7 = bf16[1,2,2,25,25]{4,3,2,1,0:T(8,128)(2,1)S(1)} copy(bf16[1,2,2,25,25]{3,2,4,1,0:T(2,128)(2,1)} %bitcast.5) | data formatting | bytes 10000 | tf_op jit(solution)/shard_map/transpose | solution.py:391
  0.9 0.0 copy-start.1
  0.9 0.0 copy-start.3
  0.9 0.0 copy-start.4
  0.9 0.0 copy-done
  1.0 0.7 %copy-done.1 = bf16[1,2,16,512]{3,2,1,0:T(8,128)(2,1)S(1)} copy-done((bf16[1,2,16,512]{3,2,1,0:T(8,128)(2,1)S(1)}, bf16[1,2,16,512]{3,2,1,0:T(8,128)(2,1)}, u32[]{:S(2)}) %copy-start.1) | copy-done | bytes 32792
  1.7 0.0 copy-done.3
  1.7 0.0 copy-done.4
  1.7 0.0 copy-start.2
  1.7 0.8 %copy-done.2 = bf16[1,2,16,512]{3,2,1,0:T(8,128)(2,1)S(1)} copy-done((bf16[1,2,16,512]{3,2,1,0:T(8,128)(2,1)S(1)}, bf16[1,2,16,512]{3,2,1,0:T(8,128)(2,1)}, u32[]{:S(2)}) %copy-start.2) | copy-done | bytes 32792
  2.4 25.9 %shard_map.64 = f32[2,2,16,512]{3,2,1,0:T(8,128)S(1)} custom-call(bf16[1,2,16,512]{3,2,1,0:T(8,128)(2,1)S(1)} %copy-done.1, bf16[1,2,16,512]{3,2,1,0:T(8,128)(2,1)S(1)} %copy-done.2, bf16[4,32,128]{2,1,0:T(8,128)(2,1)S(1)} %pad.4.taps, s32[2,16,512]{2,1,0:T(8,128)S(1)} %copy-done, s32[16]{0:T(128)S(1)} %copy-done.4, f32[9,2,9]{2,1,0:T(2,128)S(1)} %bitcast.3), custom_call_target="tpu_custom_call" | custom-call | tf_op jit(solution)/shard_map/pallas_call | solution.py:401
  28.3 0.7 %copy.9 = f32[2,2,16,512]{3,2,1,0:T(8,128)} copy(f32[2,2,16,512]{3,2,1,0:T(8,128)S(1)} %shard_map.64) | data formatting | bytes 262144
  (1 shorter events, 0.0 us)
Async XLA Ops:
  0.0 0.9 %copy-start = (s32[2,16,512]{2,1,0:T(8,128)S(1)}, s32[2,16,512]{2,1,0:T(8,128)}, u32[]{:S(2)}) copy-start(s32[2,16,512]{2,1,0:T(8,128)} %index.1) | copy-start | bytes 196612
  0.9 0.8 %copy-start.1 = (bf16[1,2,16,512]{3,2,1,0:T(8,128)(2,1)S(1)}, bf16[1,2,16,512]{3,2,1,0:T(8,128)(2,1)}, u32[]{:S(2)}) copy-start(bf16[1,2,16,512]{3,2,1,0:T(8,128)(2,1)} %source.1) | copy-start | bytes 98308
  0.9 0.8 %copy-start.3 = (f32[2,9,9]{2,0,1:T(2,128)S(1)}, f32[2,9,9]{2,0,1:T(2,128)}, u32[]{:S(2)}) copy-start(f32[2,9,9]{2,0,1:T(2,128)} %param.11) | copy-start | bytes 1948
  0.9 0.8 %copy-start.4 = (s32[16]{0:T(128)S(1)}, s32[16]{0:T(128)}, u32[]{:S(2)}) copy-start(s32[16]{0:T(128)} %lags.1) | copy-start | bytes 196
  1.7 0.8 %copy-start.2 = (bf16[1,2,16,512]{3,2,1,0:T(8,128)(2,1)S(1)}, bf16[1,2,16,512]{3,2,1,0:T(8,128)(2,1)}, u32[]{:S(2)}) copy-start(bf16[1,2,16,512]{3,2,1,0:T(8,128)(2,1)} %receiver.1) | copy-start | bytes 98308
